TPU v7x, 32 devices: a whole 2x2x4 slice. The times are simulated.
32 devices in a mesh: replica: 2 (over x), tok: 16 (over z, y, core), sec: 1.
Axes of the slice: x: 2, y: 2, z: 4, core: 2. Of those that a mesh axis runs over, the one named last changes fastest.
Arguments:
- queries: bfloat16 [4096, 8192], P(('replica', 'tok'), 'sec'), parts along dimension 0, may hold values from -96 to 96
- kv_pool: bfloat16 [64, 64, 512], P(('replica', 'tok')), parts along dimension 0, may hold values from -9 to 9
- block_table: int32 [64], P('replica'), parts along dimension 0, may hold values from 0 to 31, each once
- lengths: int32 [8], P('replica'), parts along dimension 0, may hold values from 1 to 1024, 2048 in all
- tokens_ffn: bfloat16 [2048, 3584], P(('replica', 'tok'), 'sec'), parts along dimension 0, may hold values from -6 to 6
- routes: int32 [2048, 3], P(('replica', 'tok')), parts along dimension 0, may hold values from 0 to 5, all different within a row; in each aligned block of 64 rows (0 to 63, 64 to 127, ...) at most 33 rows name the same one
- route_probs: float32 [2048, 3], P(('replica', 'tok')), parts along dimension 0, may hold values from 0.1 to 1
- w_in: bfloat16 [16, 3, 3584, 2, 320], P('tok', None, 'sec'), may hold values from -0.09375 to 0.09375
- w_out: bfloat16 [16, 3, 320, 3584], P('tok', None, None, 'sec'), may hold values from -0.125 to 0.125
Outputs:
- attention: bfloat16 [4096, 8192], P(('replica', 'tok'), 'sec'), parts along dimension 0
- moe_out: bfloat16 [2048, 3584], P(('replica', 'tok'), 'sec'), parts along dimension 0
There are 2 independent parts, one for each index of `replica`. A program takes and returns all parts, laid end to end along the dimension named above; an argument that names none is the same for every part. Nothing has to cross between parts.
Inputs may be any that keep to these rules, and one draw needn't show every extreme that they name: `routes`: in every aligned block of 64 rows, no expert is named by more than 33 rows, a bound that some block reaches.
All inputs are finite; a program needn't handle non-finite values.
Results may differ from a plain program's by a relative error of at most 0.022.
Values may be sent and summed in bfloat16 or wider, within the bound.
A program may use at most 128 MiB of HBM per device.

v0:
```python
import math

import jax
import jax.numpy as jnp
from jax import lax
from jax.sharding import PartitionSpec as P

GROUP = 8


masked_score = -1e30


def attend_block(state, query_grid, query_pos, query_req, keys_vals, key_pos, key_req, scale):
    maxima, totals, summed = state
    head_dim = query_grid.shape[2]
    keys = keys_vals[:, :head_dim]
    values = keys_vals[:, head_dim:]
    scores = jnp.einsum("thd,sd->ths", query_grid, keys, preferred_element_type=jnp.float32) * scale
    visible = (query_req[:, None] == key_req[None, :]) & (key_pos[None, :] <= query_pos[:, None])
    visible = visible[:, None, :]
    fresh = jnp.maximum(maxima, jnp.max(jnp.where(visible, scores, masked_score), axis=2))
    weights = jnp.where(visible, jnp.exp(scores - fresh[:, :, None]), 0.0)
    factor = jnp.exp(maxima - fresh)
    totals = totals * factor + jnp.sum(weights, axis=2)
    summed = summed * factor[:, :, None] + jnp.einsum(
        "ths,sd->thd", weights.astype(jnp.bfloat16), values, preferred_element_type=jnp.float32
    )
    return (fresh, totals, summed)


def body(queries, kv_pool, block_table, lengths, tokens_ffn, routes, route_probs, w_in, w_out):
    page_rows = kv_pool.shape[1]
    head_dim = kv_pool.shape[2] // 2
    pages_all = block_table.shape[0]
    query_rows = queries.shape[0]
    head_count = queries.shape[1] // head_dim
    scale = 1.0 / math.sqrt(head_dim)
    ends = jnp.cumsum(lengths)
    query_pos = lax.axis_index("tok") * query_rows + jnp.arange(query_rows, dtype=jnp.int32)
    query_req = jnp.sum((query_pos[:, None] >= ends[None, :]).astype(jnp.int32), axis=1)
    page_ids = jnp.arange(pages_all, dtype=jnp.int32)
    inverse = jnp.sum(
        jnp.where(block_table[:, None] == page_ids[None, :], page_ids[:, None], 0), axis=0
    )
    query_grid = queries.reshape(query_rows, head_count, head_dim)
    in_page = jnp.arange(page_rows, dtype=jnp.int32)
    initial = (
        jnp.full((query_rows, head_count), masked_score, jnp.float32),
        jnp.zeros((query_rows, head_count), jnp.float32),
        jnp.zeros((query_rows, head_count, head_dim), jnp.float32),
    )
    state = initial
    piece = lax.all_gather(kv_pool, "tok", axis=0, tiled=True)
    count = piece.shape[0]
    group = max(1, 1024 // page_rows)
    for begin in range(0, count, group):
        size = min(group, count - begin)
        block = piece[begin : begin + size]
        logical = lax.dynamic_slice_in_dim(inverse, begin, size)
        key_pos = (logical[:, None] * page_rows + in_page[None, :]).reshape(-1)
        key_req = jnp.sum((key_pos[:, None] >= ends[None, :]).astype(jnp.int32), axis=1)
        state = attend_block(
            state,
            query_grid,
            query_pos,
            query_req,
            block.reshape(size * page_rows, 2 * head_dim),
            key_pos,
            key_req,
            scale,
        )
    maxima, totals, summed = state
    attention = (
        (summed / totals[:, :, None])
        .astype(jnp.bfloat16)
        .reshape(query_rows, head_count * head_dim)
    )
    devices_tok = lax.axis_size("tok")
    group_experts = w_in.shape[1]
    units = w_in.shape[4]
    groups = devices_tok // GROUP
    experts = group_experts * groups
    rows_here, top = routes.shape
    half_width = tokens_ffn.shape[1]
    capacity = min(rows_here, rows_here * top // experts + 1)
    flat = routes.reshape(-1)
    onehot = (flat[:, None] == jnp.arange(experts, dtype=jnp.int32)[None, :]).astype(jnp.int32)
    earlier = jnp.cumsum(onehot, axis=0) - onehot
    slot = jnp.sum(earlier * onehot, axis=1)
    destination = (flat // group_experts * capacity + slot) * group_experts + flat % group_experts
    dest_rows = destination.reshape(rows_here, top)
    slot_ids = jnp.arange(experts * capacity, dtype=jnp.int32)
    placing = jnp.any(slot_ids[:, None, None] == dest_rows[None, :, :], axis=2).astype(jnp.bfloat16)
    grouped = (
        jnp.dot(placing, tokens_ffn, preferred_element_type=jnp.float32)
        .astype(jnp.bfloat16)
        .reshape(groups, capacity, group_experts, half_width)
    )
    buffer = jnp.repeat(grouped, GROUP, axis=0)
    gate_up = w_in[0].reshape(group_experts, half_width, 2 * units)
    down = w_out[0]
    received = lax.all_to_all(buffer, "tok", split_axis=0, concat_axis=0, tiled=True)
    sources, count, local, width = received.shape
    pre = jnp.einsum(
        "snlw,lwk->snlk", received, gate_up, preferred_element_type=jnp.float32
    ).reshape(sources, count, local, 2, units)
    summed_pre = lax.psum(pre.astype(jnp.bfloat16), "sec").astype(jnp.float32)
    hidden = (jax.nn.silu(summed_pre[:, :, :, 0]) * summed_pre[:, :, :, 1]).astype(jnp.bfloat16)
    result = jnp.einsum("snlu,lud->snld", hidden, down, preferred_element_type=jnp.float32).astype(
        jnp.bfloat16
    )
    returned = lax.all_to_all(result, "tok", split_axis=0, concat_axis=0, tiled=True)
    combined = jnp.sum(
        returned.reshape(groups, GROUP, capacity, group_experts, half_width).astype(jnp.float32),
        axis=1,
    )
    picked = combined.reshape(experts * capacity, half_width)[destination].reshape(
        rows_here, top, half_width
    )
    moe_out = jnp.sum(picked * route_probs[:, :, None], axis=1).astype(jnp.bfloat16)
    return (attention, moe_out)


def solution(mesh):
    in_specs = (
        P(("replica", "tok"), "sec"),
        P(("replica", "tok"), None, None),
        P("replica"),
        P("replica"),
        P(("replica", "tok"), "sec"),
        P(("replica", "tok"), None),
        P(("replica", "tok"), None),
        P("tok", None, "sec", None, None),
        P("tok", None, None, "sec"),
    )
    out_specs = (P(("replica", "tok"), "sec"), P(("replica", "tok"), "sec"))
    return jax.shard_map(body, mesh=mesh, in_specs=in_specs, out_specs=out_specs, check_vma=False)
```

profile of v0, /device:TPU:13, one launch (start us, length us, event | category | flops | bytes accessed | tf_op | source)
XLA Modules:
  0.0 746.1 jit_solution(12144345762826570050)
XLA Ops:
  7.2 0.0 copy-start
  7.2 0.8 copy.81
  8.0 0.1 eq.91
  8.2 1.8 reduce-window.19
  10.0 0.1 slice.52
  10.1 0.1 copy.82
  10.2 0.1 copy.83
  10.3 0.1 add_bitcast_fusion
  10.4 0.1 reduce_sum.92
  10.6 0.1 copy.84
  10.6 0.7 broadcast_divide_fusion
  11.4 0.1 fusion.26
  11.5 0.0 copy-done
  11.5 1.7 convolution_convert_fusion
  13.2 3.6 reshape.373
  16.8 1.5 copy.85
  18.3 7.4 broadcast_in_dim.86
  25.6 304.4 %all_to_all.10 = bf16[16,33,3,3584]{3,1,2,0:T(8,128)(2,1)} all-to-all(bf16[16,33,3,3584]{3,1,2,0:T(8,128)(2,1)} %bitcast.77), channel_id=1, replica_groups=mesh['replica'=2,'tok'=16,'sec'=1] {'tok'}, dimensions={0} | all-to-all | bytes 22708224 | tf_op jit(solution)/shard_map/all_to_all | solution.py:103
  330.0 18.2 %convert_bitcast_fusion.1 = f32[16,33,3,640]{3,1,0,2:T(8,128)} fusion(bf16[3,3584,640,1]{1,2,3,0:T(8,128)(2,1)} %bitcast.89, bf16[16,33,3,3584]{3,1,2,0:T(8,128)(2,1)} %all_to_all.10), kind=kOutput, calls=%fused_computation.19 | convolution fusion | flops 7268659200 | bytes 29171712 | tf_op jit(solution)/shard_map/snlw,lwk->snlk/dot_general | solution.py:105
  348.2 7.1 reshape.394
  355.3 8.0 %fusion.39 = (f32[16,33,3,1,320]{4,3,1,0,2:T(1,128)S(1)}, f32[16,33,3,1,320]{4,3,1,0,2:T(1,128)S(1)}) fusion(f32[16,33,3,2,320]{4,3,1,0,2:T(2,128)} %reshape.394), kind=kLoop, calls=%fused_computation.82 | loop fusion | bytes 8110080 | tf_op jit(solution)/shard_map/slice | solution.py:109
  363.4 0.7 fusion.14
  364.1 20.0 %convert_bitcast_fusion = bf16[16,33,3,3584]{3,1,0,2:T(8,128)(2,1)S(1)} fusion(bf16[1,3,320,3584]{3,2,1,0:T(8,128)(2,1)} %param.17, bf16[16,33,3,320]{3,0,2,1:T(8,128)(2,1)S(1)} %fusion.14), kind=kOutput, calls=%fused_computation.8 | convolution fusion | flops 3638992896 | bytes 19249152 | tf_op jit(solution)/shard_map/snlu,lud->snld/dot_general | solution.py:110
  384.1 5.8 copy.91
  390.0 6.8 all-to-all-start.1
  396.8 0.0 all-gather.2.cloned.1.call-start
  396.9 0.7 all-gather.2.cloned.1.call-update
  397.5 0.0 copy-done.4
  397.6 0.1 select_reduce_fusion.2
  397.6 0.1 slice_multiply_fusion.1
  397.7 0.1 iota_add_fusion
  397.8 0.1 add.156
  397.9 0.1 add.161
  397.9 0.0 copy-done.5
  397.9 0.2 reduce-window.18
  398.1 0.1 copy.96
  398.2 0.1 div.34
  398.4 0.1 copy.95
  398.5 0.1 rem.30
  398.6 0.1 copy.94
  398.7 0.2 ne.62
  398.9 0.1 copy.97
  399.0 0.1 convert_reduce_fusion.3
  399.1 0.1 convert_reduce_fusion.2
  399.2 0.3 compare_and_fusion.1
  399.5 187.7 %all-gather.2.cloned.1.call-done = bf16[32,64,512]{2,1,0:T(8,128)(2,1)} async-done(((bf16[2,64,512]{2,1,0:T(8,128)(2,1)}), bf16[32,64,512]{2,1,0:T(8,128)(2,1)}) %all-gather.2.cloned.1.call-update) | async-done | bytes 2097168 | tf_op jit(solution)/shard_map/all_gather | solution.py:54
  587.1 1.7 fusion.40
  588.8 0.0 copy-start.3
  588.8 4.5 select_reduce_fusion.1
  593.4 7.2 select_reduce_fusion
  600.6 4.6 fusion.2
  605.2 8.1 %fusion.4 = f32[128,32]{0,1:T(8,128)S(1)} fusion(f32[128,32,1024]{2,0,1:T(8,128)} %get-tuple-element.34, f32[128,32]{0,1:T(8,128)S(1)} %get-tuple-element.21, pred[128,1024]{1,0:T(8,128)(4,1)S(1)} %get-tuple-element.28), kind=kLoop, calls=%fused_computation.11 | loop fusion | flops 16773120 | bytes 16941056 | tf_op jit(solution)/shard_map/reduce_sum | solution.py:25
  613.4 7.5 %fusion.6 = f32[128,32,256]{2,0,1:T(8,128)S(1)} fusion(f32[128,32,1024]{2,0,1:T(8,128)} %get-tuple-element.34, f32[128,32]{0,1:T(8,128)S(1)} %get-tuple-element.21, pred[128,1024]{1,0:T(8,128)(4,1)S(1)} %get-tuple-element.28, bf16[1024,512]{1,0:T(8,128)(2,1)S(1)} %bitcast.82), kind=kOutput, calls=%fused_computation.13 | convolution fusion | flops 2164260864 | bytes 21643264 | tf_op jit(solution)/shard_map/ths,sd->thd/dot_general | solution.py:26
  620.9 5.2 divide_convert_fusion
  626.1 3.2 copy.80
  629.3 2.9 copy.98
  632.2 74.8 %all-to-all-done.1 = bf16[16,33,3,3584]{3,1,2,0:T(8,128)(2,1)} async-done(((bf16[16,33,3,3584]{3,1,2,0:T(8,128)(2,1)}), bf16[16,33,3,3584]{3,1,2,0:T(8,128)(2,1)}, u32[]{:S(2)}, u32[]{:S(2)}) %all-to-all-start.1) | async-done | bytes 11354144 | tf_op jit(solution)/shard_map/all_to_all | solution.py:113
  707.0 9.1 %convert_reduce_fusion = f32[2,33,3,3584]{3,1,2,0:T(8,128)} fusion(bf16[16,33,3,3584]{3,1,2,0:T(8,128)(2,1)} %all-to-all-done.1), kind=kLoop, calls=%fused_computation.1 | loop fusion | flops 10644480 | bytes 14192640 | tf_op jit(solution)/shard_map/reduce_sum | solution.py:114
  716.1 5.7 copy.93
  721.8 4.1 reshape.375
  725.9 0.0 copy-start.1
  725.9 3.0 gather_fusion
  729.0 4.7 reshape.376
  733.7 5.3 multiply_reduce_fusion
  (18 shorter events, 0.2 us)
Async XLA Ops:
  7.2 4.3 copy-start
  390.0 7.6 %copy-start.4 = (s32[32]{0:T(128)S(1)}, s32[32]{0:T(128)}, u32[]{:S(2)}) copy-start(s32[32]{0:T(128)} %param.11) | copy-start | bytes 388
  390.0 8.0 %copy-start.5 = (s32[4]{0:T(128)S(1)}, s32[4]{0:T(128)}, u32[]{:S(2)}) copy-start(s32[4]{0:T(128)} %param.12) | copy-start | bytes 52
  390.0 8.9 %copy-start.2 = (f32[64,3]{0,1:T(4,128)S(1)}, f32[64,3]{0,1:T(4,128)}, u32[]{:S(2)}) copy-start(f32[64,3]{0,1:T(4,128)} %param.15) | copy-start | bytes 2308
  390.0 317.0 %all-to-all-start.1 = ((bf16[16,33,3,3584]{3,1,2,0:T(8,128)(2,1)}), bf16[16,33,3,3584]{3,1,2,0:T(8,128)(2,1)}, u32[]{:S(2)}, u32[]{:S(2)}) async-start(bf16[16,33,3,3584]{3,1,2,0:T(8,128)(2,1)} %copy.91), calls=%async_computation.1 | async-start | bytes 27525120 | tf_op jit(solution)/shard_map/all_to_all | solution.py:113
  396.8 190.3 %all-gather.2.cloned.1.call-start = ((), (), s32[]{:S(2)}) async-start(), calls=%async_computation.2 | async-start | bytes 2228224 | tf_op jit(solution)/shard_map/all_gather | solution.py:54
  588.8 4.5 copy-start.3
  725.9 13.1 %copy-start.1 = (bf16[64,3584]{1,0:T(8,128)(2,1)S(1)}, bf16[64,3584]{1,0:T(8,128)(2,1)}, u32[]{:S(2)}) copy-start(bf16[64,3584]{1,0:T(8,128)(2,1)} %param.13) | copy-start | bytes 1376260
Sparse Core Ops, SparseCore 0:
  399.8 187.2 all-gather.1
where the time goes:
time: 745 us; the launch traced here: 746 us
  blocking collectives  304 us (41%)
  waiting for transfers between devices  263 us (35%)
  matrix products  64.4 us (9%)
  local copies, waits for them, and re-layouts  61.3 us (8%)
  other arithmetic  31.6 us (4%)
  between operations  14.5 us (2%)
    all_to_all x1, blocking collectives, body(): lax.all_to_all(buffer, 'tok', split_axis=0, concat_axis=0, tiled=True)  304 us
    all_gather x1, waiting for transfers between devices, body(): piece = lax.all_gather(kv_pool, 'tok', axis=0, tiled=True)  188 us
    all_to_all x1, waiting for transfers between devices, body(): lax.all_to_all(result, 'tok', split_axis=0, concat_axis=0, tiled=True)  74.8 us
    dot_general x1, matrix products, body(): jnp.einsum('snlu,lud->snld', hidden, down, preferred_element_type=jnp.flo...  20 us
    dot_general x1, matrix products, body(): jnp.einsum('snlw,lwk->snlk', received, gate_up, preferred_element_type=jn...  18.2 us
  transfers between devices with their start and end apart: 2, of which 2 were waited for; matrix products, arithmetic and copies ran while one was open for 6% of the time, Pallas kernels for 0%

commit v1 on v0

--- a/solution.py
+++ b/solution.py
@@ -1,8 +1,11 @@
+import functools
 import math
 
 import jax
 import jax.numpy as jnp
 from jax import lax
+from jax.experimental import pallas as pl
+from jax.experimental.pallas import tpu as pltpu
 from jax.sharding import PartitionSpec as P
 
 GROUP = 8
@@ -122,7 +125,386 @@
     return (attention, moe_out)
 
 
+MESH = pl.DeviceIdType.MESH
+LOG2E = 1.4426950408889634
+TRANSPOSED = (((1,), (1,)), ((), ()))
+
+
+def ring_tok(pos, chips, core):
+    half = chips // 2
+    chip = jnp.where(pos < half, 2 * pos, 2 * (chips - 1 - pos) + 1)
+    return 2 * chip + core
+
+
+def fused_kernel(
+    chips,
+    group_experts,
+    units,
+    wide,
+    head_dim,
+    x_ref,
+    kv_ref,
+    comb_ref,
+    kpos_ref,
+    start_ref,
+    q_ref,
+    w_ref,
+    v_ref,
+    att_ref,
+    moe_ref,
+    xg,
+    kvg,
+    pg,
+    wbuf,
+    vbuf,
+    hid,
+    mask,
+    own,
+    px,
+    rr,
+    local_sem,
+    load_sem,
+    ring_send,
+    ring_recv,
+    pair_send,
+    pair_recv,
+    px_send,
+    px_recv,
+    rr_send,
+    rr_recv,
+):
+    rows, width = x_ref.shape
+    kv_rows = kv_ref.shape[0]
+    tok = lax.axis_index("tok")
+    core = lax.rem(tok, 2)
+    chip = tok // 2
+    zed = chip // 2
+    pos = jnp.where(lax.rem(chip, 2) == 0, zed, chips - 1 - zed)
+    sign = 1 - 2 * core
+    partner = tok + 1 - 2 * core
+    after = ring_tok(lax.rem(pos + sign + chips, chips), chips, core)
+    before = ring_tok(lax.rem(pos - sign + chips, chips), chips, core)
+
+    def mine_at(step):
+        return ring_tok(lax.rem(pos - sign * step + 2 * chips, chips), chips, core)
+
+    def other_at(step):
+        return ring_tok(lax.rem(pos + sign * step + 2 * chips, chips), chips, 1 - core)
+
+    firsts = [
+        pltpu.make_async_copy(x_ref, xg.at[tok], local_sem.at[0]),
+        pltpu.make_async_copy(kv_ref, kvg.at[pl.ds(pl.multiple_of(tok * kv_rows, kv_rows), kv_rows)], local_sem.at[1]),
+        pltpu.make_async_copy(comb_ref, pg.at[tok], local_sem.at[2]),
+    ]
+    for copy in firsts:
+        copy.start()
+    loads = []
+    for l in range(group_experts):
+        for j in range(2):
+            loads.append(
+                pltpu.make_async_copy(
+                    w_ref.at[l, j], wbuf.at[l, pl.ds(j * wide, units)], load_sem.at[l * 3 + j]
+                )
+            )
+        loads.append(
+            pltpu.make_async_copy(v_ref.at[l], vbuf.at[pl.ds(l * wide, units)], load_sem.at[l * 3 + 2])
+        )
+    for copy in loads:
+        copy.start()
+
+    barrier = pltpu.get_barrier_semaphore()
+    for device in (before, after, partner):
+        pl.semaphore_signal(barrier, inc=1, device_id={"tok": device}, device_id_type=MESH)
+    pl.semaphore_wait(barrier, 3)
+    for copy in firsts:
+        copy.wait()
+
+    pieces = 2
+    part_rows = rows // pieces
+
+    def views(block):
+        kv_at = pl.ds(pl.multiple_of(block * kv_rows, kv_rows), kv_rows)
+        out = [kvg.at[kv_at], pg.at[block]]
+        for i in range(pieces):
+            out.append(xg.at[block, pl.ds(i * part_rows, part_rows)])
+        return out
+
+    def remote(ref, send, recv, device):
+        return pltpu.make_async_remote_copy(
+            src_ref=ref,
+            dst_ref=ref,
+            send_sem=send,
+            recv_sem=recv,
+            device_id={"tok": device},
+            device_id_type=MESH,
+        )
+
+    def forward(step, wait, send):
+        for i, ref in enumerate(views(mine_at(step))):
+            if wait:
+                remote(ref, ring_send.at[step, i], ring_recv.at[step, i], after).wait_recv()
+            if send:
+                remote(ref, ring_send.at[step, i], ring_recv.at[step + 1, i], after).start()
+            remote(ref, pair_send.at[step, i], pair_recv.at[step, i], partner).start()
+
+    def take_pair(step):
+        for i, ref in enumerate(views(other_at(step))):
+            remote(ref, pair_send.at[step, i], pair_recv.at[step, i], partner).wait_recv()
+
+    first_expert = tok // GROUP * group_experts
+
+    def up(step):
+        a, b = mine_at(step), other_at(step)
+        x = jnp.concatenate([xg[a], xg[b]], axis=0)
+        scales = jnp.concatenate(
+            [jnp.transpose(pg[a])[:rows], jnp.transpose(pg[b])[:rows]], axis=0
+        )
+        lanes = lax.broadcasted_iota(jnp.int32, scales.shape, 1)
+
+        @pl.loop(0, group_experts)
+        def _(l):
+            pre = lax.dot_general(x, wbuf[l], TRANSPOSED, preferred_element_type=jnp.float32)
+            gate, upper = pre[:, :wide], pre[:, wide:]
+            scale = jnp.sum(jnp.where(lanes == first_expert + l, scales, 0.0), axis=1, keepdims=True)
+            act = (gate / (1.0 + jnp.exp(-gate)) * upper * scale).astype(jnp.bfloat16)
+            at = pl.ds(pl.multiple_of(l * wide, 128), wide)
+            hid[a, :, at] = act[:rows]
+            hid[b, :, at] = act[rows:]
+
+    forward(0, False, True)
+
+    spare = wide - units
+    if spare:
+        for l in range(group_experts):
+            for j in range(2):
+                wbuf[l, pl.ds(j * wide + units, spare)] = jnp.zeros((spare, width), wbuf.dtype)
+            vbuf[pl.ds(l * wide + units, spare)] = jnp.zeros((spare, width), vbuf.dtype)
+    key_pos = kpos_ref[...]
+    first_pos = start_ref[...]
+    query_rows = q_ref.shape[0]
+    query_pos = tok * query_rows + lax.broadcasted_iota(jnp.int32, (query_rows, 1), 0)
+    mask[...] = jnp.where((key_pos >= first_pos) & (key_pos <= query_pos), 0.0, -1e30)
+    for copy in loads:
+        copy.wait()
+
+    @pl.loop(1, chips - 1)
+    def _(step):
+        forward(step, True, True)
+        take_pair(step - 1)
+        up(step - 1)
+
+    forward(chips - 1, True, False)
+    take_pair(chips - 2)
+    up(chips - 2)
+    take_pair(chips - 1)
+    up(chips - 1)
+
+    @pl.loop(0, chips)
+    def _(step):
+        for i, ref in enumerate(views(mine_at(step))):
+            remote(ref, pair_send.at[step, i], pair_recv.at[step, i], partner).wait_send()
+
+    @pl.loop(0, chips - 1)
+    def _(step):
+        for i, ref in enumerate(views(mine_at(step))):
+            remote(ref, ring_send.at[step, i], ring_recv.at[step, i], after).wait_send()
+
+    def px_copy(step):
+        return pltpu.make_async_remote_copy(
+            src_ref=xg.at[chips + step],
+            dst_ref=px.at[step],
+            send_sem=px_send.at[step],
+            recv_sem=px_recv.at[step],
+            device_id={"tok": partner},
+            device_id_type=MESH,
+        )
+
+    halves = 2
+    cut = width // halves
+
+    def rr_copy(step, half):
+        at = pl.ds(half * cut, cut)
+        return pltpu.make_async_remote_copy(
+            src_ref=xg.at[step, :, at],
+            dst_ref=rr.at[step, :, at],
+            send_sem=rr_send.at[step, half],
+            recv_sem=rr_recv.at[step, half],
+            device_id={"tok": after},
+            device_id_type=MESH,
+        )
+
+    tile = 512 if width % 512 == 0 else 128
+
+    def down(step):
+        a, b = mine_at(step + 1), other_at(step + 1)
+        h = jnp.concatenate([hid[a], hid[b]], axis=0)
+        slot = lax.rem(step, 2)
+
+        @pl.loop(0, width // tile)
+        def _(n):
+            at = pl.ds(pl.multiple_of(n * tile, tile), tile)
+            part = jnp.dot(h, vbuf[:, at], preferred_element_type=jnp.float32)
+            own[slot, :, at] = part[:rows]
+            xg[chips + step, :, at] = part[rows:].astype(jnp.bfloat16)
+
+        px_copy(step).start()
+
+    heads = q_ref.shape[1] // head_dim
+    together = 2 if heads % 2 == 0 else 1
+    bundles = heads // together
+    log_scale = LOG2E / math.sqrt(head_dim)
+
+    def attend(bundle):
+        at = [
+            pl.ds(pl.multiple_of((bundle * together + i) * head_dim, head_dim), head_dim)
+            for i in range(together)
+        ]
+        q = jnp.concatenate([q_ref[:, a] for a in at], axis=0)
+        scores = lax.dot_general(
+            q, kvg[:, :head_dim], TRANSPOSED, preferred_element_type=jnp.float32
+        )
+        hide = mask[...]
+        scores = scores * log_scale + jnp.concatenate([hide] * together, axis=0)
+        top = jnp.max(scores, axis=1, keepdims=True)
+        weights = jnp.exp2(scores - top)
+        total = jnp.sum(weights, axis=1, keepdims=True)
+        summed = jnp.dot(
+            weights.astype(jnp.bfloat16), kvg[:, head_dim:], preferred_element_type=jnp.float32
+        )
+        result = (summed / total).astype(jnp.bfloat16)
+        for i, a in enumerate(at):
+            att_ref[:, a] = result[i * query_rows : (i + 1) * query_rows]
+
+    def pass_on(step, receive, last):
+        px_copy(step).wait_recv()
+        slot = lax.rem(step, 2)
+        for half in range(halves):
+            at = pl.ds(half * cut, cut)
+            value = own[slot, :, at] + px[step, :, at].astype(jnp.float32)
+            if receive:
+                rr_copy(step - 1, half).wait_recv()
+                value = value + rr[step - 1, :, at].astype(jnp.float32)
+            if last:
+                moe_ref[:, at] = value.astype(jnp.bfloat16)
+            else:
+                xg[step, :, at] = value.astype(jnp.bfloat16)
+                rr_copy(step, half).start()
+
+    def attend_share(step):
+        @pl.loop(step * bundles // chips, (step + 1) * bundles // chips)
+        def _(bundle):
+            attend(bundle)
+
+    down(0)
+    down(1)
+    pass_on(0, False, False)
+    attend_share(0)
+
+    @pl.loop(1, chips - 1)
+    def _(step):
+        down(step + 1)
+        pass_on(step, True, False)
+        attend_share(step)
+
+    attend_share(chips - 1)
+    pass_on(chips - 1, True, True)
+
+    @pl.loop(0, chips)
+    def _(step):
+        px_copy(step).wait_send()
+
+    @pl.loop(0, chips - 1)
+    def _(step):
+        for half in range(halves):
+            rr_copy(step, half).wait_send()
+
+
+def ring_body(queries, kv_pool, block_table, lengths, tokens_ffn, routes, route_probs, w_in, w_out):
+    devices_tok = lax.axis_size("tok")
+    chips = devices_tok // 2
+    pages_here, page_rows, kv_width = kv_pool.shape
+    head_dim = kv_width // 2
+    pages_all = block_table.shape[0]
+    keys_all = pages_all * page_rows
+    query_rows = queries.shape[0]
+    group_experts, units = w_in.shape[1], w_in.shape[4]
+    experts = group_experts * (devices_tok // GROUP)
+    rows, width = tokens_ffn.shape
+    wide = -(-units // 128) * 128
+
+    ends = jnp.cumsum(lengths)
+    page_ids = jnp.arange(pages_all, dtype=jnp.int32)
+    inverse = jnp.sum(
+        jnp.where(block_table[:, None] == page_ids[None, :], page_ids[:, None], 0), axis=0
+    )
+    in_page = jnp.arange(page_rows, dtype=jnp.int32)
+    key_pos = (inverse[:, None] * page_rows + in_page[None, :]).reshape(1, keys_all)
+    query_pos = lax.axis_index("tok") * query_rows + jnp.arange(query_rows, dtype=jnp.int32)
+    starts = jnp.max(jnp.where(query_pos[:, None] >= ends[None, :], ends[None, :], 0), axis=1)[:, None]
+
+    expert_rows = -(-experts // 8) * 8
+    token_lanes = -(-rows // 128) * 128
+    expert_ids = jnp.arange(expert_rows, dtype=jnp.int32)
+    combine = jnp.sum(
+        jnp.where(routes.T[None] == expert_ids[:, None, None], route_probs.T[None], 0.0), axis=1
+    )
+    combine = jnp.pad(combine, ((0, 0), (0, token_lanes - rows)))
+
+    gate_up = jnp.transpose(w_in[0], (0, 2, 3, 1))
+    any_spec = pl.BlockSpec(memory_space=pl.ANY)
+    vmem = pl.BlockSpec(memory_space=pltpu.VMEM)
+    dma = pltpu.SemaphoreType.DMA
+    bf16 = jnp.bfloat16
+    kernel = functools.partial(fused_kernel, chips, group_experts, units, wide, head_dim)
+    return pl.pallas_call(
+        kernel,
+        out_shape=(
+            jax.ShapeDtypeStruct(queries.shape, bf16),
+            jax.ShapeDtypeStruct(tokens_ffn.shape, bf16),
+        ),
+        in_specs=[any_spec, any_spec, any_spec, vmem, vmem, vmem, any_spec, any_spec],
+        out_specs=(vmem, vmem),
+        scratch_shapes=[
+            pltpu.VMEM((devices_tok, rows, width), bf16),
+            pltpu.VMEM((keys_all, kv_width), bf16),
+            pltpu.VMEM((devices_tok, expert_rows, token_lanes), jnp.float32),
+            pltpu.VMEM((group_experts, 2 * wide, width), bf16),
+            pltpu.VMEM((group_experts * wide, width), bf16),
+            pltpu.VMEM((devices_tok, rows, group_experts * wide), bf16),
+            pltpu.VMEM((query_rows, keys_all), jnp.float32),
+            pltpu.VMEM((2, rows, width), jnp.float32),
+            pltpu.VMEM((chips, rows, width), bf16),
+            pltpu.VMEM((chips - 1, rows, width), bf16),
+            dma((3,)),
+            dma((group_experts * 3,)),
+            dma((chips, 4)),
+            dma((chips, 4)),
+            dma((chips, 4)),
+            dma((chips, 4)),
+            dma((chips,)),
+            dma((chips,)),
+            dma((chips - 1, 2)),
+            dma((chips - 1, 2)),
+        ],
+        compiler_params=pltpu.CompilerParams(
+            collective_id=0, has_side_effects=True, vmem_limit_bytes=60 * 1024 * 1024
+        ),
+    )(
+        tokens_ffn,
+        kv_pool.reshape(pages_here * page_rows, kv_width),
+        combine,
+        key_pos,
+        starts,
+        queries,
+        gate_up,
+        w_out[0],
+    )
+
+
 def solution(mesh):
+    ring = mesh.shape["sec"] == 1 and mesh.shape["tok"] % 8 == 0
+    chosen = ring_body if ring else body
+
     in_specs = (
         P(("replica", "tok"), "sec"),
         P(("replica", "tok"), None, None),
@@ -135,4 +517,4 @@
         P("tok", None, None, "sec"),
     )
     out_specs = (P(("replica", "tok"), "sec"), P(("replica", "tok"), "sec"))
-    return jax.shard_map(body, mesh=mesh, in_specs=in_specs, out_specs=out_specs, check_vma=False)
+    return jax.shard_map(chosen, mesh=mesh, in_specs=in_specs, out_specs=out_specs, check_vma=False)

time: 745 us -> 139 us (0.19)
  the two profiles are of different devices: /device:TPU:13 before, /device:TPU:0 now
where the time goes in v1:
time: 139 us
  Pallas kernels  130 us (94%)
  local copies, waits for them, and re-layouts  5.93 us (4%)
  other arithmetic  2.45 us (2%)
    pallas_call x1, Pallas kernels, ring_body(): pl.pallas_call(kernel, out_shape=(jax.ShapeDtypeStruct(queries.shape, bf1...  130 us
    unnamed x4, local copies, waits for them, and re-layouts  3.92 us

profile of v1, /device:TPU:0, one launch (start us, length us, event | category | flops | bytes accessed | tf_op | source)
XLA Modules:
  0.0 138.7 jit_solution(16416567465263639107)
XLA Ops:
  0.6 0.7 select_reduce_fusion
  1.4 0.8 reduce-window.8
  2.2 0.1 select_reduce_fusion.2
  2.3 0.7 select_reduce_fusion.1
  3.0 0.6 pad.4.comb_ref
  3.6 0.1 iota_add_fusion
  3.7 0.7 add.38.kpos_ref
  4.4 0.7 copy.12.start_ref
  5.1 129.6 %shard_map.104 = (bf16[128,8192]{1,0:T(8,128)(2,1)}, bf16[64,3584]{1,0:T(8,128)(2,1)}) custom-call(bf16[64,3584]{1,0:T(8,128)(2,1)} %x_ref.1, bf16[128,512]{1,0:T(8,128)(2,1)} %bitcast.12, f32[8,128]{1,0:T(8,128)} %pad.4.comb_ref, s32[1,2048]{1,0:T(1,128)} %add.38.kpos_ref, s32[128,1]{1,0:T(8,128)} %copy.12.start_ref, bf16[128,8192]{1,0:T(8,128)(2,1)} %q_ref.1, ...), custom_call_target="tpu_custom_call" | custom-call | tf_op jit(solution)/shard_map/pallas_call | solution.py:459
  134.8 0.0 copy-start
  134.8 3.1 %copy.15 = bf16[128,8192]{1,0:T(8,128)(2,1)} copy(bf16[128,8192]{1,0:T(8,128)(2,1)} %get-tuple-element.4) | data formatting | bytes 4194304
  137.9 0.0 copy-done
  137.9 0.8 copy.16
  (2 shorter events, 0.0 us)
Async XLA Ops:
  134.8 3.2 %copy-start = (bf16[64,3584]{1,0:T(8,128)(2,1)S(1)}, bf16[64,3584]{1,0:T(8,128)(2,1)}, u32[]{:S(2)}) copy-start(bf16[64,3584]{1,0:T(8,128)(2,1)} %get-tuple-element.5) | copy-start | bytes 1376260

commit v2 on v1

--- a/solution.py
+++ b/solution.py
@@ -140,13 +140,14 @@
     chips,
     group_experts,
     units,
-    wide,
     head_dim,
+    page_rows,
     x_ref,
     kv_ref,
-    comb_ref,
-    kpos_ref,
-    start_ref,
+    routes_ref,
+    probs_ref,
+    table_ref,
+    lengths_ref,
     q_ref,
     w_ref,
     v_ref,
@@ -159,7 +160,12 @@
     vbuf,
     hid,
     mask,
+    keys,
+    rows_of_values,
+    vals,
     own,
+    pstage,
+    rstage,
     px,
     rr,
     local_sem,
@@ -174,7 +180,7 @@
     rr_recv,
 ):
     rows, width = x_ref.shape
-    kv_rows = kv_ref.shape[0]
+    kv_pages = kv_ref.shape[0]
     tok = lax.axis_index("tok")
     core = lax.rem(tok, 2)
     chip = tok // 2
@@ -193,8 +199,7 @@
 
     firsts = [
         pltpu.make_async_copy(x_ref, xg.at[tok], local_sem.at[0]),
-        pltpu.make_async_copy(kv_ref, kvg.at[pl.ds(pl.multiple_of(tok * kv_rows, kv_rows), kv_rows)], local_sem.at[1]),
-        pltpu.make_async_copy(comb_ref, pg.at[tok], local_sem.at[2]),
+        pltpu.make_async_copy(kv_ref, kvg.at[pl.ds(tok * kv_pages, kv_pages)], local_sem.at[1]),
     ]
     for copy in firsts:
         copy.start()
@@ -203,14 +208,24 @@
         for j in range(2):
             loads.append(
                 pltpu.make_async_copy(
-                    w_ref.at[l, j], wbuf.at[l, pl.ds(j * wide, units)], load_sem.at[l * 3 + j]
+                    w_ref.at[l, j], wbuf.at[l, pl.ds(j * units, units)], load_sem.at[l * 3 + j]
                 )
             )
         loads.append(
-            pltpu.make_async_copy(v_ref.at[l], vbuf.at[pl.ds(l * wide, units)], load_sem.at[l * 3 + 2])
+            pltpu.make_async_copy(v_ref.at[l], vbuf.at[pl.ds(l * units, units)], load_sem.at[l * 3 + 2])
         )
     for copy in loads:
         copy.start()
+
+    names = routes_ref[...]
+    probs = probs_ref[...]
+    expert_ids = lax.broadcasted_iota(jnp.int32, (pg.shape[1], rows), 0)
+    combine = jnp.zeros(expert_ids.shape, jnp.float32)
+    for k in range(names.shape[0]):
+        combine = combine + jnp.where(names[k : k + 1] == expert_ids, probs[k : k + 1], 0.0)
+    pg[tok] = jnp.concatenate(
+        [jnp.where(core == 0, combine, 0.0), jnp.where(core == 1, combine, 0.0)], axis=1
+    )
 
     barrier = pltpu.get_barrier_semaphore()
     for device in (before, after, partner):
@@ -223,8 +238,7 @@
     part_rows = rows // pieces
 
     def views(block):
-        kv_at = pl.ds(pl.multiple_of(block * kv_rows, kv_rows), kv_rows)
-        out = [kvg.at[kv_at], pg.at[block]]
+        out = [kvg.at[pl.ds(block * kv_pages, kv_pages)], pg.at[block]]
         for i in range(pieces):
             out.append(xg.at[block, pl.ds(i * part_rows, part_rows)])
         return out
@@ -254,64 +268,51 @@
     first_expert = tok // GROUP * group_experts
 
     def up(step):
-        a, b = mine_at(step), other_at(step)
+        mine, other = mine_at(step), other_at(step)
+        a = jnp.where(core == 0, mine, other)
+        b = jnp.where(core == 0, other, mine)
         x = jnp.concatenate([xg[a], xg[b]], axis=0)
-        scales = jnp.concatenate(
-            [jnp.transpose(pg[a])[:rows], jnp.transpose(pg[b])[:rows]], axis=0
-        )
-        lanes = lax.broadcasted_iota(jnp.int32, scales.shape, 1)
+        scales = pg[a] + pg[b]
+        experts_at = lax.broadcasted_iota(jnp.int32, scales.shape, 0)
 
         @pl.loop(0, group_experts)
         def _(l):
-            pre = lax.dot_general(x, wbuf[l], TRANSPOSED, preferred_element_type=jnp.float32)
-            gate, upper = pre[:, :wide], pre[:, wide:]
-            scale = jnp.sum(jnp.where(lanes == first_expert + l, scales, 0.0), axis=1, keepdims=True)
+            pre = lax.dot_general(wbuf[l], x, TRANSPOSED, preferred_element_type=jnp.float32)
+            gate, upper = pre[:units], pre[units:]
+            scale = jnp.sum(
+                jnp.where(experts_at == first_expert + l, scales, 0.0), axis=0, keepdims=True
+            )
             act = (gate / (1.0 + jnp.exp(-gate)) * upper * scale).astype(jnp.bfloat16)
-            at = pl.ds(pl.multiple_of(l * wide, 128), wide)
-            hid[a, :, at] = act[:rows]
-            hid[b, :, at] = act[rows:]
+            hid[step, pl.ds(pl.multiple_of(l * units, units), units)] = act
 
     forward(0, False, True)
 
-    spare = wide - units
-    if spare:
-        for l in range(group_experts):
-            for j in range(2):
-                wbuf[l, pl.ds(j * wide + units, spare)] = jnp.zeros((spare, width), wbuf.dtype)
-            vbuf[pl.ds(l * wide + units, spare)] = jnp.zeros((spare, width), vbuf.dtype)
-    key_pos = kpos_ref[...]
-    first_pos = start_ref[...]
     query_rows = q_ref.shape[0]
-    query_pos = tok * query_rows + lax.broadcasted_iota(jnp.int32, (query_rows, 1), 0)
+    window = mask.shape[0]
+    base = jnp.maximum(tok * query_rows + query_rows - window, 0)
+    query_pos = tok * query_rows + lax.broadcasted_iota(jnp.int32, (1, query_rows), 1)
+    first_pos = jnp.zeros_like(query_pos)
+    end = jnp.int32(0)
+    for i in range(lengths_ref.shape[0]):
+        end = end + lengths_ref[i]
+        first_pos = jnp.where(query_pos >= end, end, first_pos)
+    key_pos = base + lax.broadcasted_iota(jnp.int32, (window, 1), 0)
     mask[...] = jnp.where((key_pos >= first_pos) & (key_pos <= query_pos), 0.0, -1e30)
+    forward(1, True, True)
+    take_pair(0)
     for copy in loads:
         copy.wait()
-
-    @pl.loop(1, chips - 1)
+    up(0)
+
+    @pl.loop(2, chips - 1)
     def _(step):
         forward(step, True, True)
         take_pair(step - 1)
         up(step - 1)
 
-    forward(chips - 1, True, False)
-    take_pair(chips - 2)
-    up(chips - 2)
-    take_pair(chips - 1)
-    up(chips - 1)
-
-    @pl.loop(0, chips)
-    def _(step):
-        for i, ref in enumerate(views(mine_at(step))):
-            remote(ref, pair_send.at[step, i], pair_recv.at[step, i], partner).wait_send()
-
-    @pl.loop(0, chips - 1)
-    def _(step):
-        for i, ref in enumerate(views(mine_at(step))):
-            remote(ref, ring_send.at[step, i], ring_recv.at[step, i], after).wait_send()
-
     def px_copy(step):
         return pltpu.make_async_remote_copy(
-            src_ref=xg.at[chips + step],
+            src_ref=pstage.at[lax.rem(step, 2)],
             dst_ref=px.at[step],
             send_sem=px_send.at[step],
             recv_sem=px_recv.at[step],
@@ -325,7 +326,7 @@
     def rr_copy(step, half):
         at = pl.ds(half * cut, cut)
         return pltpu.make_async_remote_copy(
-            src_ref=xg.at[step, :, at],
+            src_ref=rstage.at[lax.rem(step, 2), :, at],
             dst_ref=rr.at[step, :, at],
             send_sem=rr_send.at[step, half],
             recv_sem=rr_recv.at[step, half],
@@ -335,17 +336,19 @@
 
     tile = 512 if width % 512 == 0 else 128
 
-    def down(step):
-        a, b = mine_at(step + 1), other_at(step + 1)
-        h = jnp.concatenate([hid[a], hid[b]], axis=0)
+    def down(step, reuse):
+        if reuse:
+            px_copy(step - 2).wait_send()
+        h = jnp.transpose(hid[lax.rem(step + 1, chips)])
         slot = lax.rem(step, 2)
 
         @pl.loop(0, width // tile)
         def _(n):
             at = pl.ds(pl.multiple_of(n * tile, tile), tile)
             part = jnp.dot(h, vbuf[:, at], preferred_element_type=jnp.float32)
-            own[slot, :, at] = part[:rows]
-            xg[chips + step, :, at] = part[rows:].astype(jnp.bfloat16)
+            first, second = part[:rows], part[rows:]
+            own[slot, :, at] = jnp.where(core == 0, first, second)
+            pstage[slot, :, at] = jnp.where(core == 0, second, first).astype(jnp.bfloat16)
 
         px_copy(step).start()
 
@@ -361,21 +364,19 @@
         ]
         q = jnp.concatenate([q_ref[:, a] for a in at], axis=0)
         scores = lax.dot_general(
-            q, kvg[:, :head_dim], TRANSPOSED, preferred_element_type=jnp.float32
+            keys[...], q, TRANSPOSED, preferred_element_type=jnp.float32
         )
         hide = mask[...]
-        scores = scores * log_scale + jnp.concatenate([hide] * together, axis=0)
-        top = jnp.max(scores, axis=1, keepdims=True)
+        scores = scores * log_scale + jnp.concatenate([hide] * together, axis=1)
+        top = jnp.max(scores, axis=0, keepdims=True)
         weights = jnp.exp2(scores - top)
-        total = jnp.sum(weights, axis=1, keepdims=True)
-        summed = jnp.dot(
-            weights.astype(jnp.bfloat16), kvg[:, head_dim:], preferred_element_type=jnp.float32
-        )
-        result = (summed / total).astype(jnp.bfloat16)
+        total = jnp.sum(weights, axis=0, keepdims=True)
+        summed = jnp.dot(vals[...], weights.astype(jnp.bfloat16), preferred_element_type=jnp.float32)
+        result = jnp.transpose(summed / total).astype(jnp.bfloat16)
         for i, a in enumerate(at):
             att_ref[:, a] = result[i * query_rows : (i + 1) * query_rows]
 
-    def pass_on(step, receive, last):
+    def pass_on(step, receive, reuse, last):
         px_copy(step).wait_recv()
         slot = lax.rem(step, 2)
         for half in range(halves):
@@ -384,45 +385,67 @@
             if receive:
                 rr_copy(step - 1, half).wait_recv()
                 value = value + rr[step - 1, :, at].astype(jnp.float32)
+            if reuse:
+                rr_copy(step - 2, half).wait_send()
             if last:
                 moe_ref[:, at] = value.astype(jnp.bfloat16)
             else:
-                xg[step, :, at] = value.astype(jnp.bfloat16)
+                rstage[slot, :, at] = value.astype(jnp.bfloat16)
                 rr_copy(step, half).start()
 
-    def attend_share(step):
-        @pl.loop(step * bundles // chips, (step + 1) * bundles // chips)
+    down(0, False)
+    forward(chips - 1, True, False)
+    pass_on(0, False, False, False)
+    down(1, False)
+    take_pair(chips - 2)
+    up(chips - 2)
+    pass_on(1, True, False, False)
+    down(2, True)
+    take_pair(chips - 1)
+    up(chips - 1)
+
+    @pl.loop(0, window // page_rows)
+    def _(i):
+        page = table_ref[base // page_rows + i]
+        block = kvg[page]
+        at = pl.ds(pl.multiple_of(i * page_rows, page_rows), page_rows)
+        keys[at, :] = block[:, :head_dim]
+        rows_of_values[at, :] = block[:, head_dim:]
+
+    vals[...] = jnp.transpose(rows_of_values[...])
+    spans = chips - 3
+
+    @pl.loop(2, chips - 1)
+    def _(step):
+        pass_on(step, True, True, False)
+        down(step + 1, True)
+
+        @pl.loop((step - 2) * bundles // spans, (step - 1) * bundles // spans)
         def _(bundle):
             attend(bundle)
 
-    down(0)
-    down(1)
-    pass_on(0, False, False)
-    attend_share(0)
-
-    @pl.loop(1, chips - 1)
-    def _(step):
-        down(step + 1)
-        pass_on(step, True, False)
-        attend_share(step)
-
-    attend_share(chips - 1)
-    pass_on(chips - 1, True, True)
+    pass_on(chips - 1, True, True, True)
+
+    for step in (chips - 2, chips - 1):
+        px_copy(step).wait_send()
+    for half in range(halves):
+        rr_copy(chips - 2, half).wait_send()
 
     @pl.loop(0, chips)
     def _(step):
-        px_copy(step).wait_send()
+        for i, ref in enumerate(views(mine_at(step))):
+            remote(ref, pair_send.at[step, i], pair_recv.at[step, i], partner).wait_send()
 
     @pl.loop(0, chips - 1)
     def _(step):
-        for half in range(halves):
-            rr_copy(step, half).wait_send()
+        for i, ref in enumerate(views(mine_at(step))):
+            remote(ref, ring_send.at[step, i], ring_recv.at[step, i], after).wait_send()
 
 
 def ring_body(queries, kv_pool, block_table, lengths, tokens_ffn, routes, route_probs, w_in, w_out):
     devices_tok = lax.axis_size("tok")
     chips = devices_tok // 2
-    pages_here, page_rows, kv_width = kv_pool.shape
+    _, page_rows, kv_width = kv_pool.shape
     head_dim = kv_width // 2
     pages_all = block_table.shape[0]
     keys_all = pages_all * page_rows
@@ -430,52 +453,41 @@
     group_experts, units = w_in.shape[1], w_in.shape[4]
     experts = group_experts * (devices_tok // GROUP)
     rows, width = tokens_ffn.shape
-    wide = -(-units // 128) * 128
-
-    ends = jnp.cumsum(lengths)
-    page_ids = jnp.arange(pages_all, dtype=jnp.int32)
-    inverse = jnp.sum(
-        jnp.where(block_table[:, None] == page_ids[None, :], page_ids[:, None], 0), axis=0
-    )
-    in_page = jnp.arange(page_rows, dtype=jnp.int32)
-    key_pos = (inverse[:, None] * page_rows + in_page[None, :]).reshape(1, keys_all)
-    query_pos = lax.axis_index("tok") * query_rows + jnp.arange(query_rows, dtype=jnp.int32)
-    starts = jnp.max(jnp.where(query_pos[:, None] >= ends[None, :], ends[None, :], 0), axis=1)[:, None]
 
     expert_rows = -(-experts // 8) * 8
-    token_lanes = -(-rows // 128) * 128
-    expert_ids = jnp.arange(expert_rows, dtype=jnp.int32)
-    combine = jnp.sum(
-        jnp.where(routes.T[None] == expert_ids[:, None, None], route_probs.T[None], 0.0), axis=1
-    )
-    combine = jnp.pad(combine, ((0, 0), (0, token_lanes - rows)))
-
+    window = min(keys_all, keys_all // 2 + query_rows)
     gate_up = jnp.transpose(w_in[0], (0, 2, 3, 1))
     any_spec = pl.BlockSpec(memory_space=pl.ANY)
     vmem = pl.BlockSpec(memory_space=pltpu.VMEM)
+    smem = pl.BlockSpec(memory_space=pltpu.SMEM)
     dma = pltpu.SemaphoreType.DMA
     bf16 = jnp.bfloat16
-    kernel = functools.partial(fused_kernel, chips, group_experts, units, wide, head_dim)
+    kernel = functools.partial(fused_kernel, chips, group_experts, units, head_dim, page_rows)
     return pl.pallas_call(
         kernel,
         out_shape=(
             jax.ShapeDtypeStruct(queries.shape, bf16),
             jax.ShapeDtypeStruct(tokens_ffn.shape, bf16),
         ),
-        in_specs=[any_spec, any_spec, any_spec, vmem, vmem, vmem, any_spec, any_spec],
+        in_specs=[any_spec, any_spec, vmem, vmem, smem, smem, vmem, any_spec, any_spec],
         out_specs=(vmem, vmem),
         scratch_shapes=[
             pltpu.VMEM((devices_tok, rows, width), bf16),
-            pltpu.VMEM((keys_all, kv_width), bf16),
-            pltpu.VMEM((devices_tok, expert_rows, token_lanes), jnp.float32),
-            pltpu.VMEM((group_experts, 2 * wide, width), bf16),
-            pltpu.VMEM((group_experts * wide, width), bf16),
-            pltpu.VMEM((devices_tok, rows, group_experts * wide), bf16),
-            pltpu.VMEM((query_rows, keys_all), jnp.float32),
+            pltpu.VMEM((pages_all, page_rows, kv_width), bf16),
+            pltpu.VMEM((devices_tok, expert_rows, 2 * rows), jnp.float32),
+            pltpu.VMEM((group_experts, 2 * units, width), bf16),
+            pltpu.VMEM((group_experts * units, width), bf16),
+            pltpu.VMEM((chips, group_experts * units, 2 * rows), bf16),
+            pltpu.VMEM((window, query_rows), jnp.float32),
+            pltpu.VMEM((window, head_dim), bf16),
+            pltpu.VMEM((window, head_dim), bf16),
+            pltpu.VMEM((head_dim, window), bf16),
             pltpu.VMEM((2, rows, width), jnp.float32),
+            pltpu.VMEM((2, rows, width), bf16),
+            pltpu.VMEM((2, rows, width), bf16),
             pltpu.VMEM((chips, rows, width), bf16),
             pltpu.VMEM((chips - 1, rows, width), bf16),
-            dma((3,)),
+            dma((2,)),
             dma((group_experts * 3,)),
             dma((chips, 4)),
             dma((chips, 4)),
@@ -491,10 +503,11 @@
         ),
     )(
         tokens_ffn,
-        kv_pool.reshape(pages_here * page_rows, kv_width),
-        combine,
-        key_pos,
-        starts,
+        kv_pool,
+        routes.T,
+        route_probs.T,
+        block_table,
+        lengths,
         queries,
         gate_up,
         w_out[0],

time: 139 us -> 116 us (0.83)
  Pallas kernels: 130 us -> 111 us
  other arithmetic: 2.45 us -> 0 us
  local copies, waits for them, and re-layouts: 5.93 us -> 3.92 us
    pallas_call x1, Pallas kernels: 130 us -> 111 us  [ring_body(): pl.pallas_call(kernel, out_shape=(jax.ShapeDtypeStruct(queries.shape, bf1...]
    reduce_sum x2 -> x0, other arithmetic: 1.45 us -> none  [the longest x1 0.75 us: ring_body(): jnp.sum(jnp.where(block_table[:, None] == page_ids[None, :], page_ids[:,...]
where the time goes in v2:
time: 116 us
  Pallas kernels  111 us (96%)
  local copies, waits for them, and re-layouts  3.92 us (3%)
    pallas_call x1, Pallas kernels, ring_body(): pl.pallas_call(kernel, out_shape=(jax.ShapeDtypeStruct(queries.shape, bf1...  111 us
    unnamed x4, local copies, waits for them, and re-layouts  3.92 us

profile of v2, /device:TPU:0, one launch (start us, length us, event | category | flops | bytes accessed | tf_op | source)
XLA Modules:
  0.0 115.9 jit_solution(15166013500586022655)
XLA Ops:
  0.6 111.3 %shard_map.104 = (bf16[128,8192]{1,0:T(8,128)(2,1)}, bf16[64,3584]{1,0:T(8,128)(2,1)}) custom-call(bf16[64,3584]{1,0:T(8,128)(2,1)} %x_ref.1, bf16[2,64,512]{2,1,0:T(8,128)(2,1)} %kv_ref.1, s32[3,64]{1,0:T(4,128)} %bitcast.8, f32[3,64]{1,0:T(4,128)} %bitcast.9, s32[32]{0:T(128)} %table_ref.1, s32[4]{0:T(128)} %lengths_ref.1, bf16[128,8192]{1,0:T(8,128)(2,1)} %q_ref.1, ...), custom_call_target="tpu_custom_call" | custom-call | tf_op jit(solution)/shard_map/pallas_call | solution.py:466
  112.0 0.0 copy-start
  112.0 3.1 %copy.13 = bf16[128,8192]{1,0:T(8,128)(2,1)} copy(bf16[128,8192]{1,0:T(8,128)(2,1)} %get-tuple-element.4) | data formatting | bytes 4194304
  115.1 0.0 copy-done
  115.1 0.8 copy.14
Async XLA Ops:
  112.0 3.2 %copy-start = (bf16[64,3584]{1,0:T(8,128)(2,1)S(1)}, bf16[64,3584]{1,0:T(8,128)(2,1)}, u32[]{:S(2)}) copy-start(bf16[64,3584]{1,0:T(8,128)(2,1)} %get-tuple-element.5) | copy-start | bytes 1376260

commit v3 on v2

--- a/solution.py
+++ b/solution.py
@@ -312,7 +312,7 @@
 
     def px_copy(step):
         return pltpu.make_async_remote_copy(
-            src_ref=pstage.at[lax.rem(step, 2)],
+            src_ref=pstage.at[step],
             dst_ref=px.at[step],
             send_sem=px_send.at[step],
             recv_sem=px_recv.at[step],
@@ -326,7 +326,7 @@
     def rr_copy(step, half):
         at = pl.ds(half * cut, cut)
         return pltpu.make_async_remote_copy(
-            src_ref=rstage.at[lax.rem(step, 2), :, at],
+            src_ref=rstage.at[step, :, at],
             dst_ref=rr.at[step, :, at],
             send_sem=rr_send.at[step, half],
             recv_sem=rr_recv.at[step, half],
@@ -336,9 +336,7 @@
 
     tile = 512 if width % 512 == 0 else 128
 
-    def down(step, reuse):
-        if reuse:
-            px_copy(step - 2).wait_send()
+    def down(step):
         h = jnp.transpose(hid[lax.rem(step + 1, chips)])
         slot = lax.rem(step, 2)
 
@@ -348,7 +346,7 @@
             part = jnp.dot(h, vbuf[:, at], preferred_element_type=jnp.float32)
             first, second = part[:rows], part[rows:]
             own[slot, :, at] = jnp.where(core == 0, first, second)
-            pstage[slot, :, at] = jnp.where(core == 0, second, first).astype(jnp.bfloat16)
+            pstage[step, :, at] = jnp.where(core == 0, second, first).astype(jnp.bfloat16)
 
         px_copy(step).start()
 
@@ -376,7 +374,7 @@
         for i, a in enumerate(at):
             att_ref[:, a] = result[i * query_rows : (i + 1) * query_rows]
 
-    def pass_on(step, receive, reuse, last):
+    def pass_on(step, receive, last):
         px_copy(step).wait_recv()
         slot = lax.rem(step, 2)
         for half in range(halves):
@@ -385,22 +383,20 @@
             if receive:
                 rr_copy(step - 1, half).wait_recv()
                 value = value + rr[step - 1, :, at].astype(jnp.float32)
-            if reuse:
-                rr_copy(step - 2, half).wait_send()
             if last:
                 moe_ref[:, at] = value.astype(jnp.bfloat16)
             else:
-                rstage[slot, :, at] = value.astype(jnp.bfloat16)
+                rstage[step, :, at] = value.astype(jnp.bfloat16)
                 rr_copy(step, half).start()
 
-    down(0, False)
+    down(0)
     forward(chips - 1, True, False)
-    pass_on(0, False, False, False)
-    down(1, False)
+    pass_on(0, False, False)
+    down(1)
     take_pair(chips - 2)
     up(chips - 2)
-    pass_on(1, True, False, False)
-    down(2, True)
+    pass_on(1, True, False)
+    down(2)
     take_pair(chips - 1)
     up(chips - 1)
 
@@ -417,19 +413,23 @@
 
     @pl.loop(2, chips - 1)
     def _(step):
-        pass_on(step, True, True, False)
-        down(step + 1, True)
+        pass_on(step, True, False)
+        down(step + 1)
 
         @pl.loop((step - 2) * bundles // spans, (step - 1) * bundles // spans)
         def _(bundle):
             attend(bundle)
 
-    pass_on(chips - 1, True, True, True)
-
-    for step in (chips - 2, chips - 1):
+    pass_on(chips - 1, True, True)
+
+    @pl.loop(0, chips)
+    def _(step):
         px_copy(step).wait_send()
-    for half in range(halves):
-        rr_copy(chips - 2, half).wait_send()
+
+    @pl.loop(0, chips - 1)
+    def _(step):
+        for half in range(halves):
+            rr_copy(step, half).wait_send()
 
     @pl.loop(0, chips)
     def _(step):
@@ -483,8 +483,8 @@
             pltpu.VMEM((window, head_dim), bf16),
             pltpu.VMEM((head_dim, window), bf16),
             pltpu.VMEM((2, rows, width), jnp.float32),
-            pltpu.VMEM((2, rows, width), bf16),
-            pltpu.VMEM((2, rows, width), bf16),
+            pltpu.VMEM((chips, rows, width), bf16),
+            pltpu.VMEM((chips - 1, rows, width), bf16),
             pltpu.VMEM((chips, rows, width), bf16),
             pltpu.VMEM((chips - 1, rows, width), bf16),
             dma((2,)),

time: 116 us -> 116 us (level)
  no operation moved by 1% of the time
where the time goes in v3:
time: 116 us
  Pallas kernels  111 us (96%)
  local copies, waits for them, and re-layouts  3.92 us (3%)
    pallas_call x1, Pallas kernels, ring_body(): pl.pallas_call(kernel, out_shape=(jax.ShapeDtypeStruct(queries.shape, bf1...  111 us
    unnamed x4, local copies, waits for them, and re-layouts  3.92 us

profile of v3, /device:TPU:0, one launch (start us, length us, event | category | flops | bytes accessed | tf_op | source)
XLA Modules:
  0.0 115.8 jit_solution(3957394057925441416)
XLA Ops:
  0.6 111.3 %shard_map.104 = (bf16[128,8192]{1,0:T(8,128)(2,1)}, bf16[64,3584]{1,0:T(8,128)(2,1)}) custom-call(bf16[64,3584]{1,0:T(8,128)(2,1)} %x_ref.1, bf16[2,64,512]{2,1,0:T(8,128)(2,1)} %kv_ref.1, s32[3,64]{1,0:T(4,128)} %bitcast.8, f32[3,64]{1,0:T(4,128)} %bitcast.9, s32[32]{0:T(128)} %table_ref.1, s32[4]{0:T(128)} %lengths_ref.1, bf16[128,8192]{1,0:T(8,128)(2,1)} %q_ref.1, ...), custom_call_target="tpu_custom_call" | custom-call | tf_op jit(solution)/shard_map/pallas_call | solution.py:466
  111.9 0.0 copy-start
  111.9 3.1 %copy.13 = bf16[128,8192]{1,0:T(8,128)(2,1)} copy(bf16[128,8192]{1,0:T(8,128)(2,1)} %get-tuple-element.4) | data formatting | bytes 4194304
  115.1 0.0 copy-done
  115.1 0.8 copy.14
Async XLA Ops:
  111.9 3.2 %copy-start = (bf16[64,3584]{1,0:T(8,128)(2,1)S(1)}, bf16[64,3584]{1,0:T(8,128)(2,1)}, u32[]{:S(2)}) copy-start(bf16[64,3584]{1,0:T(8,128)(2,1)} %get-tuple-element.5) | copy-start | bytes 1376260
